TPU v7x, 32 devices: a whole 2x2x4 slice. The times are simulated.
32 devices in a mesh: parts: 2 (over y), outer: 4 (over x, core), blk: 4 (over z).
Axes of the slice: x: 2, y: 2, z: 4, core: 2. Of those that a mesh axis runs over, the one named last changes fastest.
Arguments:
- q_teacher: bfloat16 [4096, 512], P(('parts', 'outer', 'blk')), parts along dimension 0, may hold values from -30 to 30
- k_teacher: bfloat16 [4096, 512], P(('parts', 'outer', 'blk')), parts along dimension 0, may hold values from -30 to 30
- q_student: bfloat16 [4096, 512], P(('parts', 'outer', 'blk')), parts along dimension 0, may hold values from -30 to 30
- k_student: bfloat16 [4096, 512], P(('parts', 'outer', 'blk')), parts along dimension 0, may hold values from -30 to 30
- positions: int32 [4096], P(('parts', 'outer', 'blk')), parts along dimension 0, may hold values from 0 to 511, as said below
Outputs:
- grad_query: float32 [4096, 512], P(('parts', 'outer', 'blk')), parts along dimension 0
- grad_key: float32 [4096, 512], P(('parts', 'outer', 'blk')), parts along dimension 0
There are 2 independent parts, one for each index of `parts`. A program takes and returns all parts, laid end to end along the dimension named above; each array names one. Nothing has to cross between parts.
Inputs may be any that keep to these rules, and one draw needn't show every extreme that they name: `positions`: positions count 0, 1, 2, ... from the first token of each document; documents are 64 to 512 tokens long (the last may be cut by the sequence's end) and one is exactly 512 long.
All inputs are finite; a program needn't handle non-finite values.
Results may differ from a plain program's by a relative error of at most 0.0085.
Values may be sent and summed in bfloat16 or wider, within the bound.
A program may use at most 64 MiB of HBM per device.

v0:
```python
import jax
import jax.numpy as jnp
from jax import lax
from jax.sharding import PartitionSpec as P

HEADS = 4
HEAD_DIM = 128
LOSS_SCALE = 256


LOWEST = -1e30


def shifted(array, axis, by):
    length = lax.axis_size(axis)
    pairs = [(i, i + by) for i in range(length) if 0 <= i + by < length]
    return lax.ppermute(array, axis, pairs)


def passed_along(block, axis, distance):
    devices = range(lax.axis_size(axis))
    route = [((i - distance) % len(devices), i) for i in devices]
    return lax.ppermute(block, axis, route)


def split_heads(matrix):
    return matrix.reshape(matrix.shape[0], HEADS, HEAD_DIM)


def visible(query_index, query_low, key_index):
    return (key_index[None, :] <= query_index[:, None]) & (key_index[None, :] >= query_low[:, None])


def head_scores(query_heads, key_heads):
    return jnp.einsum(
        "qhd,khd->hqk", query_heads, key_heads, preferred_element_type=jnp.float32
    ) * HEAD_DIM ** (-0.5)


def online_update(carried, scores, is_seen, values):
    top_old, total_old, accum_old = carried
    masked = jnp.where(is_seen[None], scores, -jnp.inf)
    top_new = jnp.maximum(top_old, jnp.max(masked, axis=2))
    weights = jnp.where(is_seen[None], jnp.exp(scores - top_new[:, :, None]), 0.0)
    fade = jnp.exp(top_old - top_new)
    total_new = total_old * fade + jnp.sum(weights, axis=2)
    accum_new = accum_old * fade[:, :, None] + jnp.einsum(
        "hqk,khd->hqd", weights.astype(jnp.bfloat16), values, preferred_element_type=jnp.float32
    )
    return (top_new, total_new, accum_new)


def body(q_teacher, k_teacher, q_student, k_student, positions):
    row_count = q_teacher.shape[0]
    width = q_teacher.shape[1]
    cycle_size = lax.axis_size("blk")
    outer_size = lax.axis_size("outer")
    me_outer = lax.axis_index("outer")
    me_blk = lax.axis_index("blk")
    offsets = jnp.arange(row_count, dtype=jnp.int32)
    q_index = (me_outer * cycle_size + me_blk) * row_count + offsets
    q_low = q_index - positions
    inv_root = HEAD_DIM ** (-0.5)
    query_heads = (split_heads(q_teacher), split_heads(q_student))
    key_heads = (split_heads(k_teacher), split_heads(k_student))

    def block_index(group_id, source):
        return (group_id * cycle_size + source) * row_count + offsets

    def absorb(carried, key_pair, key_index, in_range):
        is_seen = visible(q_index, q_low, key_index) & in_range
        teacher_keys = split_heads(key_pair[0])
        student_keys = split_heads(key_pair[1])
        teacher_part = online_update(
            carried[0], head_scores(query_heads[0], teacher_keys), is_seen, student_keys
        )
        student_part = online_update(
            carried[1], head_scores(query_heads[1], student_keys), is_seen, student_keys
        )
        return (teacher_part, student_part)

    empty_side = (
        jnp.full((HEADS, row_count), LOWEST, jnp.float32),
        jnp.zeros((HEADS, row_count), jnp.float32),
        jnp.zeros((HEADS, row_count, HEAD_DIM), jnp.float32),
    )
    carried = (empty_side, empty_side)
    keys_own = jnp.stack([k_teacher, k_student])
    keys_prior = shifted(keys_own, "outer", 1)
    prior_ok = me_outer >= 1

    def key_circle(carried, key_pair, group_id, in_range):
        carried = absorb(carried, key_pair, block_index(group_id, me_blk), in_range)

        def key_cycle_turn(step_number, carry):
            held_state, moving = carry
            moving = passed_along(moving, "blk", 1)
            source = (me_blk - step_number) % cycle_size
            return (absorb(held_state, moving, block_index(group_id, source), in_range), moving)

        carried, spent = lax.fori_loop(1, cycle_size, key_cycle_turn, (carried, key_pair))
        return carried

    carried = key_circle(carried, keys_own, me_outer, True)
    carried = key_circle(carried, keys_prior, me_outer - 1, prior_ok)
    (teacher_top, teacher_total, teacher_accum), (student_top, student_total, student_accum) = (
        carried
    )
    grad_heads = (
        LOSS_SCALE
        * inv_root
        * (student_accum / student_total[:, :, None] - teacher_accum / teacher_total[:, :, None])
    )
    grad_query = jnp.transpose(grad_heads, (1, 0, 2)).reshape(row_count, width)
    teacher_lse = teacher_top + jnp.log(teacher_total)
    student_lse = student_top + jnp.log(student_total)
    row_stats = jnp.concatenate([teacher_lse, student_lse, q_low.astype(jnp.float32)[None]], 0)
    queries_own = jnp.stack([q_teacher, q_student])
    queries_later = shifted(queries_own, "outer", -1)
    stats_later = shifted(row_stats, "outer", -1)
    later_ok = me_outer + 1 < outer_size
    key_index_own = block_index(me_outer, me_blk)

    def emit(grad_keys, query_pair, query_stats, query_index, in_range):
        query_low = query_stats[2 * HEADS].astype(jnp.int32)
        is_seen = visible(query_index, query_low, key_index_own) & in_range
        teacher_q = split_heads(query_pair[0])
        student_q = split_heads(query_pair[1])
        teacher_prob = jnp.where(
            is_seen[None],
            jnp.exp(head_scores(teacher_q, key_heads[0]) - query_stats[:HEADS][:, :, None]),
            0.0,
        )
        student_prob = jnp.where(
            is_seen[None],
            jnp.exp(
                head_scores(student_q, key_heads[1]) - query_stats[HEADS : 2 * HEADS][:, :, None]
            ),
            0.0,
        )
        score_grad = (LOSS_SCALE * (student_prob - teacher_prob)).astype(jnp.bfloat16)
        return grad_keys + inv_root * jnp.einsum(
            "hqk,qhd->khd", score_grad, student_q, preferred_element_type=jnp.float32
        )

    grad_keys = jnp.zeros((row_count, HEADS, HEAD_DIM), jnp.float32)

    def query_circle(grad_keys, query_pair, query_stats, group_id, in_range):
        grad_keys = emit(
            grad_keys, query_pair, query_stats, block_index(group_id, me_blk), in_range
        )

        def query_cycle_turn(step_number, carry):
            held_grad, moving_pair, moving_stats = carry
            moving_pair = passed_along(moving_pair, "blk", 1)
            moving_stats = passed_along(moving_stats, "blk", 1)
            source = (me_blk - step_number) % cycle_size
            held_grad = emit(
                held_grad, moving_pair, moving_stats, block_index(group_id, source), in_range
            )
            return (held_grad, moving_pair, moving_stats)

        grad_keys, spent_pair, spent_stats = lax.fori_loop(
            1, cycle_size, query_cycle_turn, (grad_keys, query_pair, query_stats)
        )
        return grad_keys

    grad_keys = query_circle(grad_keys, queries_own, row_stats, me_outer, True)
    grad_keys = query_circle(grad_keys, queries_later, stats_later, me_outer + 1, later_ok)
    return (grad_query, grad_keys.reshape(row_count, width))


def solution(mesh):
    in_specs = (
        P(("parts", "outer", "blk"), None),
        P(("parts", "outer", "blk"), None),
        P(("parts", "outer", "blk"), None),
        P(("parts", "outer", "blk"), None),
        P(("parts", "outer", "blk")),
    )
    out_specs = (P(("parts", "outer", "blk"), None), P(("parts", "outer", "blk"), None))
    return jax.shard_map(body, mesh=mesh, in_specs=in_specs, out_specs=out_specs, check_vma=False)
```

profile of v0, /device:TPU:0, one launch (start us, length us, event | category | flops | bytes accessed | tf_op | source)
XLA Modules:
  0.0 148.4 jit_solution(12706113307877614306)
XLA Ops:
  2.6 2.5 %collective-permute-start.6 = (bf16[2,128,512]{1,2,0:T(8,128)(2,1)}, bf16[2,128,512]{1,2,0:T(8,128)(2,1)S(1)}, u32[]{:S(2)}, u32[]{:S(2)}) collective-permute-start(bf16[2,128,512]{1,2,0:T(8,128)(2,1)} %pad_maximum_fusion), channel_id=1, source_target_pairs={{0,4},{4,8},{8,12},{1,5},{5,9},{9,13},{2,6},{6,10},{10,14},{3,7},{... | collective-permute-start | bytes 786440 | tf_op jit(solution)/shard_map/ppermute | solution.py:17
  11.9 37.3 %while.96 = (s32[]{:T(128)}, f32[4,128]{1,0:T(4,128)S(1)}, f32[4,128]{1,0:T(4,128)S(1)}, f32[4,128,128]{2,1,0:T(8,128)S(1)}, f32[4,128]{1,0:T(4,128)S(1)}, /*ind...) while((s32[]{:T(128)}, f32[4,128]{1,0:T(4,128)S(1)}, ...), condition=%wide.region_9.10_spmd.clone, body=%wide.region_4.9_spmd.clone.sunk | while | flops 68602128 | bytes 5917550 | solution.py:101
  11.9 2.5 %collective-permute-start = (bf16[2,128,512]{1,2,0:T(8,128)(2,1)}, bf16[2,128,512]{1,2,0:T(8,128)(2,1)S(1)}, u32[]{:S(2)}, u32[]{:S(2)}) collective-permute-start(bf16[2,128,512]{1,2,0:T(8,128)(2,1)} %get-tuple-element.1983), channel_id=1, source_target_pairs={{3,0},{0,1},{1,2},{2,3},{7,4},{4,5},{5,6},{6,7},{11,8},{8,9},{9,10... | collective-permute-start | bytes 786440 | tf_op jit(solution)/shard_map/while/body/eval_jaxpr/ppermute | solution.py:23
  14.5 7.5 %collective-permute-done = bf16[2,128,512]{1,2,0:T(8,128)(2,1)S(1)} collective-permute-done((bf16[2,128,512]{1,2,0:T(8,128)(2,1)}, bf16[2,128,512]{1,2,0:T(8,128)(2,1)S(1)}, u32[]{:S(2)}, u32[]{:S(2)}) %collective-permute-start) | collective-permute-done | bytes 262176 | tf_op jit(solution)/shard_map/while/body/eval_jaxpr/ppermute | solution.py:23
  24.4 10.2 %collective-permute-done = bf16[2,128,512]{1,2,0:T(8,128)(2,1)S(1)} collective-permute-done((bf16[2,128,512]{1,2,0:T(8,128)(2,1)}, bf16[2,128,512]{1,2,0:T(8,128)(2,1)S(1)}, u32[]{:S(2)}, u32[]{:S(2)}) %collective-permute-start) | collective-permute-done | bytes 262176 | tf_op jit(solution)/shard_map/while/body/eval_jaxpr/ppermute | solution.py:23
  36.7 10.5 %collective-permute-done = bf16[2,128,512]{1,2,0:T(8,128)(2,1)S(1)} collective-permute-done((bf16[2,128,512]{1,2,0:T(8,128)(2,1)}, bf16[2,128,512]{1,2,0:T(8,128)(2,1)S(1)}, u32[]{:S(2)}, u32[]{:S(2)}) %collective-permute-start) | collective-permute-done | bytes 262176 | tf_op jit(solution)/shard_map/while/body/eval_jaxpr/ppermute | solution.py:23
  50.9 30.4 %while.97 = (s32[]{:T(128)}, f32[4,128]{1,0:T(4,128)S(1)}, f32[4,128]{1,0:T(4,128)S(1)}, f32[4,128,128]{2,1,0:T(8,128)S(1)}, f32[4,128]{1,0:T(4,128)S(1)}, /*ind...) while((s32[]{:T(128)}, f32[4,128]{1,0:T(4,128)S(1)}, ...), condition=%wide.region_19.20_spmd.clone, body=%wide.region_14.19_spmd.clone.sunk | while | flops 68618512 | bytes 5917559 | solution.py:101
  51.0 9.5 %collective-permute-done.1 = bf16[2,128,512]{1,2,0:T(8,128)(2,1)S(1)} collective-permute-done((bf16[2,128,512]{1,2,0:T(8,128)(2,1)S(1)}, bf16[2,128,512]{1,2,0:T(8,128)(2,1)S(1)}, u32[]{:S(2)}, u32[]{:S(2)}) %collective-permute-start.1) | collective-permute-done | bytes 262176 | tf_op jit(solution)/shard_map/while/body/eval_jaxpr/ppermute | solution.py:23
  62.0 8.5 %collective-permute-done.1 = bf16[2,128,512]{1,2,0:T(8,128)(2,1)S(1)} collective-permute-done((bf16[2,128,512]{1,2,0:T(8,128)(2,1)S(1)}, bf16[2,128,512]{1,2,0:T(8,128)(2,1)S(1)}, u32[]{:S(2)}, u32[]{:S(2)}) %collective-permute-start.1) | collective-permute-done | bytes 262176 | tf_op jit(solution)/shard_map/while/body/eval_jaxpr/ppermute | solution.py:23
  72.0 8.0 %collective-permute-done.1 = bf16[2,128,512]{1,2,0:T(8,128)(2,1)S(1)} collective-permute-done((bf16[2,128,512]{1,2,0:T(8,128)(2,1)S(1)}, bf16[2,128,512]{1,2,0:T(8,128)(2,1)S(1)}, u32[]{:S(2)}, u32[]{:S(2)}) %collective-permute-start.1) | collective-permute-done | bytes 262176 | tf_op jit(solution)/shard_map/while/body/eval_jaxpr/ppermute | solution.py:23
  85.8 34.2 %while.98 = (s32[]{:T(128)}, f32[128,4,128]{2,0,1:T(8,128)S(1)}, bf16[2,128,512]{1,2,0:T(8,128)(2,1)}, f32[9,128]{1,0:T(8,128)S(1)}, s32[]{:T(128)}, /*index=5*/...) while((s32[]{:T(128)}, f32[128,4,128]{2,0,1:T(8,128)S(1)}, ...), condition=%wide.region_21.22_spmd.clone, body=%wide.region_20.21_spmd.clone.sunk | while | flops 51102096 | bytes 3763054 | solution.py:163
  85.9 5.4 %collective-permute-done.3 = f32[9,128]{1,0:T(8,128)S(1)} collective-permute-done((f32[9,128]{1,0:T(8,128)S(1)}, f32[9,128]{1,0:T(8,128)S(1)}, u32[]{:S(2)}, u32[]{:S(2)}) %collective-permute-start.3) | collective-permute-done | bytes 4640 | tf_op jit(solution)/shard_map/while/body/eval_jaxpr/ppermute | solution.py:23
  91.4 5.1 %collective-permute-done.2 = bf16[2,128,512]{1,2,0:T(8,128)(2,1)S(1)} collective-permute-done((bf16[2,128,512]{1,2,0:T(8,128)(2,1)}, bf16[2,128,512]{1,2,0:T(8,128)(2,1)S(1)}, u32[]{:S(2)}, u32[]{:S(2)}) %collective-permute-start.2) | collective-permute-done | bytes 262176 | tf_op jit(solution)/shard_map/while/body/eval_jaxpr/ppermute | solution.py:23
  98.3 5.2 %collective-permute-done.3 = f32[9,128]{1,0:T(8,128)S(1)} collective-permute-done((f32[9,128]{1,0:T(8,128)S(1)}, f32[9,128]{1,0:T(8,128)S(1)}, u32[]{:S(2)}, u32[]{:S(2)}) %collective-permute-start.3) | collective-permute-done | bytes 4640 | tf_op jit(solution)/shard_map/while/body/eval_jaxpr/ppermute | solution.py:23
  103.6 4.3 %collective-permute-done.2 = bf16[2,128,512]{1,2,0:T(8,128)(2,1)S(1)} collective-permute-done((bf16[2,128,512]{1,2,0:T(8,128)(2,1)}, bf16[2,128,512]{1,2,0:T(8,128)(2,1)S(1)}, u32[]{:S(2)}, u32[]{:S(2)}) %collective-permute-start.2) | collective-permute-done | bytes 262176 | tf_op jit(solution)/shard_map/while/body/eval_jaxpr/ppermute | solution.py:23
  109.7 5.2 %collective-permute-done.3 = f32[9,128]{1,0:T(8,128)S(1)} collective-permute-done((f32[9,128]{1,0:T(8,128)S(1)}, f32[9,128]{1,0:T(8,128)S(1)}, u32[]{:S(2)}, u32[]{:S(2)}) %collective-permute-start.3) | collective-permute-done | bytes 4640 | tf_op jit(solution)/shard_map/while/body/eval_jaxpr/ppermute | solution.py:23
  115.1 3.4 %collective-permute-done.2 = bf16[2,128,512]{1,2,0:T(8,128)(2,1)S(1)} collective-permute-done((bf16[2,128,512]{1,2,0:T(8,128)(2,1)}, bf16[2,128,512]{1,2,0:T(8,128)(2,1)S(1)}, u32[]{:S(2)}, u32[]{:S(2)}) %collective-permute-start.2) | collective-permute-done | bytes 262176 | tf_op jit(solution)/shard_map/while/body/eval_jaxpr/ppermute | solution.py:23
  120.3 27.3 %while.99 = (s32[]{:T(128)}, f32[128,4,128]{2,0,1:T(8,128)S(1)}, bf16[2,128,512]{1,2,0:T(8,128)(2,1)S(1)}, f32[9,128]{1,0:T(8,128)S(1)}, s32[]{:T(128)}, /*index...) while((s32[]{:T(128)}, f32[128,4,128]{2,0,1:T(8,128)S(1)}, ...), condition=%wide.region_23.24_spmd.clone, body=%wide.region_22.23_spmd.clone.sunk | while | flops 51118480 | bytes 3763063 | solution.py:163
  120.8 5.0 %collective-permute-done.5 = f32[9,128]{1,0:T(8,128)S(1)} collective-permute-done((f32[9,128]{1,0:T(8,128)S(1)}, f32[9,128]{1,0:T(8,128)S(1)}, u32[]{:S(2)}, u32[]{:S(2)}) %collective-permute-start.5) | collective-permute-done | bytes 4640 | tf_op jit(solution)/shard_map/while/body/eval_jaxpr/ppermute | solution.py:23
  125.9 2.7 %collective-permute-done.4 = bf16[2,128,512]{1,2,0:T(8,128)(2,1)S(1)} collective-permute-done((bf16[2,128,512]{1,2,0:T(8,128)(2,1)S(1)}, bf16[2,128,512]{1,2,0:T(8,128)(2,1)S(1)}, u32[]{:S(2)}, u32[]{:S(2)}) %collective-permute-start.4) | collective-permute-done | bytes 262176 | tf_op jit(solution)/shard_map/while/body/eval_jaxpr/ppermute | solution.py:23
  130.4 4.5 %collective-permute-done.5 = f32[9,128]{1,0:T(8,128)S(1)} collective-permute-done((f32[9,128]{1,0:T(8,128)S(1)}, f32[9,128]{1,0:T(8,128)S(1)}, u32[]{:S(2)}, u32[]{:S(2)}) %collective-permute-start.5) | collective-permute-done | bytes 4640 | tf_op jit(solution)/shard_map/while/body/eval_jaxpr/ppermute | solution.py:23
  135.1 2.7 %collective-permute-done.4 = bf16[2,128,512]{1,2,0:T(8,128)(2,1)S(1)} collective-permute-done((bf16[2,128,512]{1,2,0:T(8,128)(2,1)S(1)}, bf16[2,128,512]{1,2,0:T(8,128)(2,1)S(1)}, u32[]{:S(2)}, u32[]{:S(2)}) %collective-permute-start.4) | collective-permute-done | bytes 262176 | tf_op jit(solution)/shard_map/while/body/eval_jaxpr/ppermute | solution.py:23
  139.9 4.2 %collective-permute-done.5 = f32[9,128]{1,0:T(8,128)S(1)} collective-permute-done((f32[9,128]{1,0:T(8,128)S(1)}, f32[9,128]{1,0:T(8,128)S(1)}, u32[]{:S(2)}, u32[]{:S(2)}) %collective-permute-start.5) | collective-permute-done | bytes 4640 | tf_op jit(solution)/shard_map/while/body/eval_jaxpr/ppermute | solution.py:23
  144.2 2.7 %collective-permute-done.4 = bf16[2,128,512]{1,2,0:T(8,128)(2,1)S(1)} collective-permute-done((bf16[2,128,512]{1,2,0:T(8,128)(2,1)S(1)}, bf16[2,128,512]{1,2,0:T(8,128)(2,1)S(1)}, u32[]{:S(2)}, u32[]{:S(2)}) %collective-permute-start.4) | collective-permute-done | bytes 262176 | tf_op jit(solution)/shard_map/while/body/eval_jaxpr/ppermute | solution.py:23
  (233 shorter events, 36.9 us)
Async XLA Ops:
  1.8 3.2 %copy-start.4 = (bf16[128,512]{1,0:T(8,128)(2,1)S(1)}, bf16[128,512]{1,0:T(8,128)(2,1)}, u32[]{:S(2)}) copy-start(bf16[128,512]{1,0:T(8,128)(2,1)} %param.13) | copy-start | bytes 393220
  2.6 2.6 %copy-start.5 = (bf16[128,512]{1,0:T(8,128)(2,1)S(1)}, bf16[128,512]{1,0:T(8,128)(2,1)}, u32[]{:S(2)}) copy-start(bf16[128,512]{1,0:T(8,128)(2,1)} %param.15) | copy-start | bytes 393220
  2.6 8.0 %collective-permute-start.6 = (bf16[2,128,512]{1,2,0:T(8,128)(2,1)}, bf16[2,128,512]{1,2,0:T(8,128)(2,1)S(1)}, u32[]{:S(2)}, u32[]{:S(2)}) collective-permute-start(bf16[2,128,512]{1,2,0:T(8,128)(2,1)} %pad_maximum_fusion), channel_id=1, source_target_pairs={{0,4},{4,8},{8,12},{1,5},{5,9},{9,13},{2,6},{6,10},{10,14},{3,7},{... | collective-permute-start | bytes 786440 | tf_op jit(solution)/shard_map/ppermute | solution.py:17
  5.3 2.0 %copy-start = (bf16[128,512]{1,0:T(8,128)(2,1)S(1)}, bf16[128,512]{1,0:T(8,128)(2,1)}, u32[]{:S(2)}) copy-start(bf16[128,512]{1,0:T(8,128)(2,1)} %param.14) | copy-start | bytes 393220
  6.1 77.5 %collective-permute-start.7 = (bf16[2,128,512]{1,2,0:T(8,128)(2,1)}, bf16[2,128,512]{1,2,0:T(8,128)(2,1)S(1)}, u32[]{:S(2)}, u32[]{:S(2)}) collective-permute-start(bf16[2,128,512]{1,2,0:T(8,128)(2,1)} %pad_maximum_fusion.1), channel_id=1, source_target_pairs={{4,0},{8,4},{12,8},{5,1},{9,5},{13,9},{6,2},{10,6},{14,10},{7,3},{... | collective-permute-start | bytes 786440 | tf_op jit(solution)/shard_map/ppermute | solution.py:17
  11.9 10.1 %collective-permute-start = (bf16[2,128,512]{1,2,0:T(8,128)(2,1)}, bf16[2,128,512]{1,2,0:T(8,128)(2,1)S(1)}, u32[]{:S(2)}, u32[]{:S(2)}) collective-permute-start(bf16[2,128,512]{1,2,0:T(8,128)(2,1)} %get-tuple-element.1983), channel_id=1, source_target_pairs={{3,0},{0,1},{1,2},{2,3},{7,4},{4,5},{5,6},{6,7},{11,8},{8,9},{9,10... | collective-permute-start | bytes 786440 | tf_op jit(solution)/shard_map/while/body/eval_jaxpr/ppermute | solution.py:23
  24.0 10.6 %collective-permute-start = (bf16[2,128,512]{1,2,0:T(8,128)(2,1)}, bf16[2,128,512]{1,2,0:T(8,128)(2,1)S(1)}, u32[]{:S(2)}, u32[]{:S(2)}) collective-permute-start(bf16[2,128,512]{1,2,0:T(8,128)(2,1)} %get-tuple-element.1983), channel_id=1, source_target_pairs={{3,0},{0,1},{1,2},{2,3},{7,4},{4,5},{5,6},{6,7},{11,8},{8,9},{9,10... | collective-permute-start | bytes 786440 | tf_op jit(solution)/shard_map/while/body/eval_jaxpr/ppermute | solution.py:23
  36.6 10.6 %collective-permute-start = (bf16[2,128,512]{1,2,0:T(8,128)(2,1)}, bf16[2,128,512]{1,2,0:T(8,128)(2,1)S(1)}, u32[]{:S(2)}, u32[]{:S(2)}) collective-permute-start(bf16[2,128,512]{1,2,0:T(8,128)(2,1)} %get-tuple-element.1983), channel_id=1, source_target_pairs={{3,0},{0,1},{1,2},{2,3},{7,4},{4,5},{5,6},{6,7},{11,8},{8,9},{9,10... | collective-permute-start | bytes 786440 | tf_op jit(solution)/shard_map/while/body/eval_jaxpr/ppermute | solution.py:23
  50.9 9.6 %collective-permute-start.1 = (bf16[2,128,512]{1,2,0:T(8,128)(2,1)S(1)}, bf16[2,128,512]{1,2,0:T(8,128)(2,1)S(1)}, u32[]{:S(2)}, u32[]{:S(2)}) collective-permute-start(bf16[2,128,512]{1,2,0:T(8,128)(2,1)S(1)} %get-tuple-element.2041), channel_id=1, source_target_pairs={{3,0},{0,1},{1,2},{2,3},{7,4},{4,5},{5,6},{6,7},{11,8},{8,9},{9,10... | collective-permute-start | bytes 786440 | tf_op jit(solution)/shard_map/while/body/eval_jaxpr/ppermute | solution.py:23
  61.8 8.7 %collective-permute-start.1 = (bf16[2,128,512]{1,2,0:T(8,128)(2,1)S(1)}, bf16[2,128,512]{1,2,0:T(8,128)(2,1)S(1)}, u32[]{:S(2)}, u32[]{:S(2)}) collective-permute-start(bf16[2,128,512]{1,2,0:T(8,128)(2,1)S(1)} %get-tuple-element.2041), channel_id=1, source_target_pairs={{3,0},{0,1},{1,2},{2,3},{7,4},{4,5},{5,6},{6,7},{11,8},{8,9},{9,10... | collective-permute-start | bytes 786440 | tf_op jit(solution)/shard_map/while/body/eval_jaxpr/ppermute | solution.py:23
  71.8 8.2 %collective-permute-start.1 = (bf16[2,128,512]{1,2,0:T(8,128)(2,1)S(1)}, bf16[2,128,512]{1,2,0:T(8,128)(2,1)S(1)}, u32[]{:S(2)}, u32[]{:S(2)}) collective-permute-start(bf16[2,128,512]{1,2,0:T(8,128)(2,1)S(1)} %get-tuple-element.2041), channel_id=1, source_target_pairs={{3,0},{0,1},{1,2},{2,3},{7,4},{4,5},{5,6},{6,7},{11,8},{8,9},{9,10... | collective-permute-start | bytes 786440 | tf_op jit(solution)/shard_map/while/body/eval_jaxpr/ppermute | solution.py:23
  81.4 3.1 %collective-permute-start.8 = (f32[9,128]{1,0:T(8,128)S(1)}, f32[9,128]{1,0:T(8,128)S(1)}, u32[]{:S(2)}, u32[]{:S(2)}) collective-permute-start(f32[9,128]{1,0:T(8,128)S(1)} %pad_maximum_fusion.2), channel_id=1, source_target_pairs={{4,0},{8,4},{12,8},{5,1},{9,5},{13,9},{6,2},{10,6},{14,10},{7,3},{... | collective-permute-start | bytes 13832 | tf_op jit(solution)/shard_map/ppermute | solution.py:17
  85.8 5.5 %collective-permute-start.3 = (f32[9,128]{1,0:T(8,128)S(1)}, f32[9,128]{1,0:T(8,128)S(1)}, u32[]{:S(2)}, u32[]{:S(2)}) collective-permute-start(f32[9,128]{1,0:T(8,128)S(1)} %get-tuple-element.2091), channel_id=1, source_target_pairs={{3,0},{0,1},{1,2},{2,3},{7,4},{4,5},{5,6},{6,7},{11,8},{8,9},{9,10... | collective-permute-start | bytes 13832 | tf_op jit(solution)/shard_map/while/body/eval_jaxpr/ppermute | solution.py:23
  85.8 10.7 %collective-permute-start.2 = (bf16[2,128,512]{1,2,0:T(8,128)(2,1)}, bf16[2,128,512]{1,2,0:T(8,128)(2,1)S(1)}, u32[]{:S(2)}, u32[]{:S(2)}) collective-permute-start(bf16[2,128,512]{1,2,0:T(8,128)(2,1)} %get-tuple-element.2090), channel_id=1, source_target_pairs={{3,0},{0,1},{1,2},{2,3},{7,4},{4,5},{5,6},{6,7},{11,8},{8,9},{9,10... | collective-permute-start | bytes 786440 | tf_op jit(solution)/shard_map/while/body/eval_jaxpr/ppermute | solution.py:23
  98.0 5.6 %collective-permute-start.3 = (f32[9,128]{1,0:T(8,128)S(1)}, f32[9,128]{1,0:T(8,128)S(1)}, u32[]{:S(2)}, u32[]{:S(2)}) collective-permute-start(f32[9,128]{1,0:T(8,128)S(1)} %get-tuple-element.2091), channel_id=1, source_target_pairs={{3,0},{0,1},{1,2},{2,3},{7,4},{4,5},{5,6},{6,7},{11,8},{8,9},{9,10... | collective-permute-start | bytes 13832 | tf_op jit(solution)/shard_map/while/body/eval_jaxpr/ppermute | solution.py:23
  98.0 9.9 %collective-permute-start.2 = (bf16[2,128,512]{1,2,0:T(8,128)(2,1)}, bf16[2,128,512]{1,2,0:T(8,128)(2,1)S(1)}, u32[]{:S(2)}, u32[]{:S(2)}) collective-permute-start(bf16[2,128,512]{1,2,0:T(8,128)(2,1)} %get-tuple-element.2090), channel_id=1, source_target_pairs={{3,0},{0,1},{1,2},{2,3},{7,4},{4,5},{5,6},{6,7},{11,8},{8,9},{9,10... | collective-permute-start | bytes 786440 | tf_op jit(solution)/shard_map/while/body/eval_jaxpr/ppermute | solution.py:23
  109.3 5.6 %collective-permute-start.3 = (f32[9,128]{1,0:T(8,128)S(1)}, f32[9,128]{1,0:T(8,128)S(1)}, u32[]{:S(2)}, u32[]{:S(2)}) collective-permute-start(f32[9,128]{1,0:T(8,128)S(1)} %get-tuple-element.2091), channel_id=1, source_target_pairs={{3,0},{0,1},{1,2},{2,3},{7,4},{4,5},{5,6},{6,7},{11,8},{8,9},{9,10... | collective-permute-start | bytes 13832 | tf_op jit(solution)/shard_map/while/body/eval_jaxpr/ppermute | solution.py:23
  109.4 9.1 %collective-permute-start.2 = (bf16[2,128,512]{1,2,0:T(8,128)(2,1)}, bf16[2,128,512]{1,2,0:T(8,128)(2,1)S(1)}, u32[]{:S(2)}, u32[]{:S(2)}) collective-permute-start(bf16[2,128,512]{1,2,0:T(8,128)(2,1)} %get-tuple-element.2090), channel_id=1, source_target_pairs={{3,0},{0,1},{1,2},{2,3},{7,4},{4,5},{5,6},{6,7},{11,8},{8,9},{9,10... | collective-permute-start | bytes 786440 | tf_op jit(solution)/shard_map/while/body/eval_jaxpr/ppermute | solution.py:23
  120.3 5.5 %collective-permute-start.5 = (f32[9,128]{1,0:T(8,128)S(1)}, f32[9,128]{1,0:T(8,128)S(1)}, u32[]{:S(2)}, u32[]{:S(2)}) collective-permute-start(f32[9,128]{1,0:T(8,128)S(1)} %get-tuple-element.2134), channel_id=1, source_target_pairs={{3,0},{0,1},{1,2},{2,3},{7,4},{4,5},{5,6},{6,7},{11,8},{8,9},{9,10... | collective-permute-start | bytes 13832 | tf_op jit(solution)/shard_map/while/body/eval_jaxpr/ppermute | solution.py:23
  120.4 8.2 %collective-permute-start.4 = (bf16[2,128,512]{1,2,0:T(8,128)(2,1)S(1)}, bf16[2,128,512]{1,2,0:T(8,128)(2,1)S(1)}, u32[]{:S(2)}, u32[]{:S(2)}) collective-permute-start(bf16[2,128,512]{1,2,0:T(8,128)(2,1)S(1)} %get-tuple-element.2133), channel_id=1, source_target_pairs={{3,0},{0,1},{1,2},{2,3},{7,4},{4,5},{5,6},{6,7},{11,8},{8,9},{9,10... | collective-permute-start | bytes 786440 | tf_op jit(solution)/shard_map/while/body/eval_jaxpr/ppermute | solution.py:23
  129.4 5.5 %collective-permute-start.5 = (f32[9,128]{1,0:T(8,128)S(1)}, f32[9,128]{1,0:T(8,128)S(1)}, u32[]{:S(2)}, u32[]{:S(2)}) collective-permute-start(f32[9,128]{1,0:T(8,128)S(1)} %get-tuple-element.2134), channel_id=1, source_target_pairs={{3,0},{0,1},{1,2},{2,3},{7,4},{4,5},{5,6},{6,7},{11,8},{8,9},{9,10... | collective-permute-start | bytes 13832 | tf_op jit(solution)/shard_map/while/body/eval_jaxpr/ppermute | solution.py:23
  129.5 8.2 %collective-permute-start.4 = (bf16[2,128,512]{1,2,0:T(8,128)(2,1)S(1)}, bf16[2,128,512]{1,2,0:T(8,128)(2,1)S(1)}, u32[]{:S(2)}, u32[]{:S(2)}) collective-permute-start(bf16[2,128,512]{1,2,0:T(8,128)(2,1)S(1)} %get-tuple-element.2133), channel_id=1, source_target_pairs={{3,0},{0,1},{1,2},{2,3},{7,4},{4,5},{5,6},{6,7},{11,8},{8,9},{9,10... | collective-permute-start | bytes 786440 | tf_op jit(solution)/shard_map/while/body/eval_jaxpr/ppermute | solution.py:23
  138.5 5.5 %collective-permute-start.5 = (f32[9,128]{1,0:T(8,128)S(1)}, f32[9,128]{1,0:T(8,128)S(1)}, u32[]{:S(2)}, u32[]{:S(2)}) collective-permute-start(f32[9,128]{1,0:T(8,128)S(1)} %get-tuple-element.2134), channel_id=1, source_target_pairs={{3,0},{0,1},{1,2},{2,3},{7,4},{4,5},{5,6},{6,7},{11,8},{8,9},{9,10... | collective-permute-start | bytes 13832 | tf_op jit(solution)/shard_map/while/body/eval_jaxpr/ppermute | solution.py:23
  138.6 8.2 %collective-permute-start.4 = (bf16[2,128,512]{1,2,0:T(8,128)(2,1)S(1)}, bf16[2,128,512]{1,2,0:T(8,128)(2,1)S(1)}, u32[]{:S(2)}, u32[]{:S(2)}) collective-permute-start(bf16[2,128,512]{1,2,0:T(8,128)(2,1)S(1)} %get-tuple-element.2133), channel_id=1, source_target_pairs={{3,0},{0,1},{1,2},{2,3},{7,4},{4,5},{5,6},{6,7},{11,8},{8,9},{9,10... | collective-permute-start | bytes 786440 | tf_op jit(solution)/shard_map/while/body/eval_jaxpr/ppermute | solution.py:23
  (4 other events, 3.4 us)
where the time goes:
time: 149 us; the launch traced here: 148 us
  waiting for transfers between devices  105 us (70%)
  matrix products  13.8 us (9%)
  starting transfers between devices  11.6 us (8%)
  local copies, waits for them, and re-layouts  10 us (7%)
  other arithmetic  5.7 us (4%)
    ppermute x18, waiting for transfers between devices, passed_along(): return lax.ppermute(block, axis, route)  105 us
    ppermute x18, starting transfers between devices, passed_along(): return lax.ppermute(block, axis, route)  6.52 us
    dot_general x23, matrix products, head_scores(): jnp.einsum('qhd,khd->hqk', query_heads, key_heads, preferred_element_type...  5.97 us
    ppermute x3, starting transfers between devices, shifted(): return lax.ppermute(array, axis, pairs)  5.06 us
    dot_general x16, matrix products, online_update(): jnp.einsum('hqk,khd->hqd', weights.astype(jnp.bfloat16), values, preferre...  4.39 us
    while x30, local copies, waits for them, and re-layouts  4.33 us
    unnamed x22, local copies, waits for them, and re-layouts  3.93 us
    dot_general x8, matrix products, emit(): jnp.einsum('hqk,qhd->khd', score_grad, student_q, preferred_element_type=...  3.42 us
  transfers between devices with their start and end apart: 21, of which 19 were waited for; matrix products, arithmetic and copies ran while one was open for 11% of the time, Pallas kernels for 0%

commit v1 on v0

v1 whole, which is shorter than its diff:
```python
import functools
import math

import jax
import jax.numpy as jnp
from jax import lax
from jax.experimental import pallas as pl
from jax.experimental.pallas import tpu as pltpu
from jax.sharding import PartitionSpec as P

HEADS = 4
HEAD_DIM = 128
LOSS_SCALE = 256
LOWEST = -1e30
INV_ROOT = HEAD_DIM ** (-0.5)
MESH = pl.DeviceIdType.MESH


def kernel(
    blk, total, rows,
    qt_ref, kt_ref, qs_ref, ks_ref, pos_ref,
    dq_ref, dk_ref,
    ktb, ksb, qtb, qsb, posb,
    acc, dq_out, dq_in, dk_out, dk_in, part_out, part_in,
    local_sem, send_sem, recv_sem, fsend, frecv, psend, precv,
    dqs, dqr, dks, dkr,
):
    prior = blk // HEADS
    team_rows = HEADS * rows
    own = prior * team_rows
    window = own + rows
    o = lax.axis_index("outer")
    z = lax.axis_index("blk")
    line = o * blk + z
    r = lax.rem(z, HEADS)
    z0 = z - r

    def at(index):
        return {"outer": index // blk, "blk": lax.rem(index, blk)}

    def mate(place):
        return {"outer": o, "blk": z0 + place}

    barrier = pltpu.get_barrier_semaphore()
    for k in range(1, HEADS):
        pl.semaphore_signal(
            barrier, inc=1, device_id=mate(lax.rem(r + k, HEADS)), device_id_type=MESH
        )
    for p in range(1, prior + 1):
        @pl.when(line >= HEADS * p)
        def _():
            pl.semaphore_signal(
                barrier, inc=1, device_id=at(line - HEADS * p), device_id_type=MESH
            )

        @pl.when(line + HEADS * p < total)
        def _():
            pl.semaphore_signal(
                barrier, inc=1, device_id=at(line + HEADS * p), device_id_type=MESH
            )

    def slab(place):
        return pl.ds(pl.multiple_of(place * rows, rows), rows)

    def cols(place):
        return pl.ds(pl.multiple_of(place * HEAD_DIM, HEAD_DIM), HEAD_DIM)

    def own_slab(place):
        return pl.ds(pl.multiple_of(own + place * rows, rows), rows)

    def routes(head, place):
        return (
            (kt_ref.at[:, cols(head)], ktb.at[own_slab(place), :]),
            (ks_ref.at[:, cols(head)], ksb.at[own_slab(place), :]),
            (qt_ref.at[:, cols(head)], qtb.at[slab(place), :]),
            (qs_ref.at[:, cols(head)], qsb.at[slab(place), :]),
            (pos_ref, posb.at[place]),
        )

    locals_ = [
        pltpu.make_async_copy(src, dst, local_sem.at[a])
        for a, (src, dst) in enumerate(routes(r, r))
    ]
    for copy in locals_:
        copy.start()

    for p in range(1, prior + 1):
        @pl.when(line < HEADS * p)
        def _():
            lo = (prior - p) * team_rows
            ktb[lo : lo + team_rows, :] = jnp.zeros((team_rows, HEAD_DIM), jnp.bfloat16)
            ksb[lo : lo + team_rows, :] = jnp.zeros((team_rows, HEAD_DIM), jnp.bfloat16)

    before = jnp.minimum(line // HEADS, prior)
    after = jnp.minimum((total - 1 - line) // HEADS, prior)
    pl.semaphore_wait(barrier, HEADS - 1 + before + after)

    def outgoing(k, a):
        place = lax.rem(r + k, HEADS)
        src, dst = routes(place, r)[a]
        return pltpu.make_async_remote_copy(
            src_ref=src, dst_ref=dst, send_sem=send_sem.at[k - 1, a], recv_sem=recv_sem.at[r, a],
            device_id=mate(place), device_id_type=MESH,
        )

    def incoming(k, a):
        place = lax.rem(r + k, HEADS)
        src, dst = routes(r, place)[a]
        return pltpu.make_async_remote_copy(
            src_ref=src, dst_ref=dst, send_sem=send_sem.at[k - 1, a],
            recv_sem=recv_sem.at[place, a],
            device_id=mate(place), device_id_type=MESH,
        )

    for group in ((0, 1), (2, 3, 4)):
        for k in range(1, HEADS):
            for a in group:
                outgoing(k, a).start()

    def forward(p, k, a, target):
        place = lax.rem(r + k, HEADS)
        buf = (ktb, ksb)[a]
        there = pl.ds(
            pl.multiple_of((prior - p) * team_rows + place * rows, rows), rows
        )
        return pltpu.make_async_remote_copy(
            src_ref=buf.at[own_slab(place), :], dst_ref=buf.at[there, :],
            send_sem=fsend.at[p - 1, place, a], recv_sem=frecv.at[p - 1, place, a],
            device_id=at(target), device_id_type=MESH,
        )

    def forward_all(k):
        for p in range(1, prior + 1):
            @pl.when(line + HEADS * p < total)
            def _():
                for a in range(2):
                    forward(p, k, a, line + HEADS * p).start()

    locals_[0].wait()
    locals_[1].wait()
    forward_all(0)
    acc[...] = jnp.zeros_like(acc)
    for copy in locals_[2:]:
        copy.wait()
    for k in range(1, HEADS):
        incoming(k, 0).wait_recv()
        incoming(k, 1).wait_recv()
        forward_all(k)
    for k in range(1, HEADS):
        for a in (2, 3, 4):
            incoming(k, a).wait_recv()
    for p in range(1, prior + 1):
        @pl.when(line >= HEADS * p)
        def _():
            for k in range(HEADS):
                for a in range(2):
                    forward(p, k, a, line - HEADS * p).wait_recv()

    def send_part(block, target):
        p = prior - block // HEADS
        j = block % HEADS
        return pltpu.make_async_remote_copy(
            src_ref=part_out.at[block], dst_ref=part_in.at[p - 1, j],
            send_sem=psend.at[block], recv_sem=precv.at[p - 1, j],
            device_id=at(target), device_id_type=MESH,
        )

    def return_part(block):
        p = prior - block // HEADS

        @pl.when(line >= HEADS * p)
        def _():
            part_out[block] = acc[block * rows : (block + 1) * rows, :].astype(jnp.bfloat16)
            send_part(block, line - HEADS * p).start()

    def result(out, into, send, recv, place, head):
        return pltpu.make_async_remote_copy(
            src_ref=out.at[place], dst_ref=into.at[head],
            send_sem=send.at[place], recv_sem=recv.at[head],
            device_id=mate(place), device_id_type=MESH,
        )

    def give(i, value, ref, out, into, send, recv):
        @pl.when(r == i)
        def _():
            ref[:, cols(r)] = value

        @pl.when(r != i)
        def _():
            out[i] = value.astype(jnp.bfloat16)
            result(out, into, send, recv, i, r).start()

    ahead = lax.broadcasted_iota(jnp.int32, (window, rows), 0) - lax.broadcasted_iota(
        jnp.int32, (window, rows), 1
    ) - own
    power = INV_ROOT * math.log2(math.e)

    def weights(keys, queries, seen):
        scores = lax.dot_general(
            keys, queries, (((1,), (1,)), ((), ())), preferred_element_type=jnp.float32
        )
        masked = jnp.where(seen, scores, LOWEST)
        top = jnp.max(masked, axis=0, keepdims=True)
        raised = jnp.exp2((masked - top) * power)
        return raised, LOSS_SCALE / jnp.sum(raised, axis=0, keepdims=True)

    for i in range(HEADS):
        lo = i * rows
        seen = (ahead <= 0) & (ahead >= -posb[i])
        queries = qsb[lo : lo + rows, :]
        keys = ksb[lo : lo + window, :]
        t_raised, t_scale = weights(ktb[lo : lo + window, :], qtb[lo : lo + rows, :], seen)
        s_raised, s_scale = weights(keys, queries, seen)
        grad = (s_raised * s_scale - t_raised * t_scale).astype(jnp.bfloat16)
        acc[lo : lo + window, :] += jnp.dot(
            grad, queries, preferred_element_type=jnp.float32
        ) * INV_ROOT
        return_part(i)
        dq = lax.dot_general(
            grad, keys, (((0,), (0,)), ((), ())), preferred_element_type=jnp.float32
        ) * INV_ROOT
        give(i, dq, dq_ref, dq_out, dq_in, dqs, dqr)
    for block in range(HEADS, blk):
        return_part(block)

    for j in range(HEADS):
        for p in range(1, prior + 1):
            @pl.when(line + HEADS * p < total)
            def _():
                send_part((prior - p) * HEADS + j, line + HEADS * p).wait_recv()
                lo = own + j * rows
                acc[lo : lo + rows, :] += part_in[p - 1, j].astype(jnp.float32)
        give(
            j, acc[own + j * rows : own + (j + 1) * rows, :], dk_ref, dk_out, dk_in, dks, dkr
        )

    for ref, out, into, send, recv in (
        (dq_ref, dq_out, dq_in, dqs, dqr),
        (dk_ref, dk_out, dk_in, dks, dkr),
    ):
        for k in range(1, HEADS):
            place = lax.rem(r + k, HEADS)
            result(out, into, send, recv, place, place).wait_recv()
            ref[:, cols(place)] = into[place].astype(jnp.float32)

    for k in range(1, HEADS):
        for a in range(5):
            outgoing(k, a).wait_send()
        place = lax.rem(r + k, HEADS)
        result(dq_out, dq_in, dqs, dqr, place, r).wait_send()
        result(dk_out, dk_in, dks, dkr, place, r).wait_send()
    for p in range(1, prior + 1):
        @pl.when(line + HEADS * p < total)
        def _():
            for k in range(HEADS):
                for a in range(2):
                    forward(p, k, a, line + HEADS * p).wait_send()

        @pl.when(line >= HEADS * p)
        def _():
            for j in range(HEADS):
                send_part((prior - p) * HEADS + j, line - HEADS * p).wait_send()


def body(q_teacher, k_teacher, q_student, k_student, positions):
    rows, width = q_teacher.shape
    blk = lax.axis_size("blk")
    total = lax.axis_size("outer") * blk
    prior = blk // HEADS
    span = (blk + HEADS) * rows
    bf16, f32 = jnp.bfloat16, jnp.float32
    tile = (rows, HEAD_DIM)
    dma = pltpu.SemaphoreType.DMA
    pairs = HEADS * (span * rows) * HEAD_DIM
    return pl.pallas_call(
        functools.partial(kernel, blk, total, rows),
        out_shape=[jax.ShapeDtypeStruct((rows, width), f32)] * 2,
        in_specs=[pl.BlockSpec(memory_space=pl.ANY)] * 5,
        out_specs=[pl.BlockSpec(memory_space=pltpu.VMEM)] * 2,
        scratch_shapes=[
            pltpu.VMEM((span, HEAD_DIM), bf16),
            pltpu.VMEM((span, HEAD_DIM), bf16),
            pltpu.VMEM((HEADS * rows, HEAD_DIM), bf16),
            pltpu.VMEM((HEADS * rows, HEAD_DIM), bf16),
            pltpu.VMEM((HEADS, 1, rows), jnp.int32),
            pltpu.VMEM((span, HEAD_DIM), f32),
            pltpu.VMEM((HEADS,) + tile, bf16),
            pltpu.VMEM((HEADS,) + tile, bf16),
            pltpu.VMEM((HEADS,) + tile, bf16),
            pltpu.VMEM((HEADS,) + tile, bf16),
            pltpu.VMEM((blk,) + tile, bf16),
            pltpu.VMEM((prior, HEADS) + tile, bf16),
            dma((5,)),
            dma((HEADS - 1, 5)),
            dma((HEADS, 5)),
            dma((prior, HEADS, 2)),
            dma((prior, HEADS, 2)),
            dma((blk,)),
            dma((prior, HEADS)),
            dma((HEADS,)),
            dma((HEADS,)),
            dma((HEADS,)),
            dma((HEADS,)),
        ],
        compiler_params=pltpu.CompilerParams(
            collective_id=0, has_side_effects=True, vmem_limit_bytes=32 * 1024 * 1024
        ),
        cost_estimate=pl.CostEstimate(
            flops=8 * pairs, bytes_accessed=10 * rows * width * 2, transcendentals=2 * pairs // HEAD_DIM
        ),
    )(q_teacher, k_teacher, q_student, k_student, positions.reshape(1, rows))


def solution(mesh):
    spec = P(("parts", "outer", "blk"), None)
    return jax.shard_map(
        body,
        mesh=mesh,
        in_specs=(spec, spec, spec, spec, P(("parts", "outer", "blk"))),
        out_specs=(spec, spec),
        check_vma=False,
    )
```

time: 149 us -> 32.6 us (0.22)
  waiting for transfers between devices: 105 us -> 0 us
  Pallas kernels: 0 us -> 26.1 us
  matrix products: 13.8 us -> 0 us
  starting transfers between devices: 11.6 us -> 0 us
  other arithmetic: 5.7 us -> 0 us
  local copies, waits for them, and re-layouts: 10 us -> 5.67 us
    ppermute x21 -> x0, waiting for transfers between devices: 105 us -> none  [the longest x18 105 us: passed_along(): return lax.ppermute(block, axis, route)]
    pallas_call x0 -> x1, Pallas kernels: none -> 26.1 us  [body(): pl.pallas_call(functools.partial(kernel, blk, total, rows), out_shape=[ja...]
    dot_general x47 -> x0, matrix products: 13.8 us -> none  [the longest x23 5.97 us: head_scores(): jnp.einsum('qhd,khd->hqk', query_heads, key_heads, preferred_element_type...]
    ppermute x21 -> x0, starting transfers between devices: 11.6 us -> none  [the longest x18 6.52 us: passed_along(): return lax.ppermute(block, axis, route)]
    while x30 -> x0, local copies, waits for them, and re-layouts: 4.33 us -> none
    unnamed x22 -> x12, local copies, waits for them, and re-layouts: 3.93 us -> 5.67 us
    reduce_sum x8 -> x0, other arithmetic: 1.5 us -> none  [online_update(): total_new = total_old * fade + jnp.sum(weights, axis=2)]
  transfers between devices with their start and end apart: 21 -> 0, of which waited for: 19 -> 0; matrix products, arithmetic and copies ran while one was open for 11% -> 0% of each run, Pallas kernels for 0% -> 0%
where the time goes in v1:
time: 32.6 us; the launch traced here: 32.4 us
  Pallas kernels  26.1 us (80%)
  local copies, waits for them, and re-layouts  5.67 us (17%)
  between operations  0.65 us (2%)
    pallas_call x1, Pallas kernels, body(): pl.pallas_call(functools.partial(kernel, blk, total, rows), out_shape=[ja...  26.1 us
    unnamed x12, local copies, waits for them, and re-layouts  5.67 us

profile of v1, /device:TPU:0, one launch (start us, length us, event | category | flops | bytes accessed | tf_op | source)
XLA Modules:
  0.0 32.4 jit_solution(4287654518878934243)
XLA Ops:
  0.6 0.0 copy-start.4
  0.6 0.6 %copy-done.4 = s32[128]{0:T(128)S(1)} copy-done((s32[128]{0:T(128)S(1)}, s32[128]{0:T(128)}, u32[]{:S(2)}) %copy-start.4) | copy-done | bytes 536
  1.3 0.0 copy-start
  1.3 0.9 %copy-done = bf16[128,512]{1,0:T(8,128)(2,1)S(1)} copy-done((bf16[128,512]{1,0:T(8,128)(2,1)S(1)}, bf16[128,512]{1,0:T(8,128)(2,1)}, u32[]{:S(2)}) %copy-start) | copy-done | bytes 131096
  2.2 0.0 copy-start.1
  2.2 0.9 %copy-done.1 = bf16[128,512]{1,0:T(8,128)(2,1)S(1)} copy-done((bf16[128,512]{1,0:T(8,128)(2,1)S(1)}, bf16[128,512]{1,0:T(8,128)(2,1)}, u32[]{:S(2)}) %copy-start.1) | copy-done | bytes 131096
  3.1 0.0 copy-start.2
  3.1 0.9 %copy-done.2 = bf16[128,512]{1,0:T(8,128)(2,1)S(1)} copy-done((bf16[128,512]{1,0:T(8,128)(2,1)S(1)}, bf16[128,512]{1,0:T(8,128)(2,1)}, u32[]{:S(2)}) %copy-start.2) | copy-done | bytes 131096
  4.0 0.0 copy-start.3
  4.0 0.9 %copy-done.3 = bf16[128,512]{1,0:T(8,128)(2,1)S(1)} copy-done((bf16[128,512]{1,0:T(8,128)(2,1)S(1)}, bf16[128,512]{1,0:T(8,128)(2,1)}, u32[]{:S(2)}) %copy-start.3) | copy-done | bytes 131096
  4.9 26.1 %shard_map.68 = (f32[128,512]{1,0:T(8,128)S(1)}, f32[128,512]{1,0:T(8,128)S(1)}) custom-call(bf16[128,512]{1,0:T(8,128)(2,1)S(1)} %copy-done, bf16[128,512]{1,0:T(8,128)(2,1)S(1)} %copy-done.1, bf16[128,512]{1,0:T(8,128)(2,1)S(1)} %copy-done.2, bf16[128,512]{1,0:T(8,128)(2,1)S(1)} %copy-done.3, s32[1,128]{1,0:T(1,128)S(1)} %bitcast.1), custom_call_target="tpu_custom_call" | custom-call | flops 536870912 | bytes 1310720 | tf_op jit(solution)/shard_map/pallas_call | solution.py:275
  31.0 0.7 %copy.9 = f32[128,512]{1,0:T(8,128)} copy(f32[128,512]{1,0:T(8,128)S(1)} %get-tuple-element.4) | data formatting | bytes 524288
  31.7 0.7 %copy.10 = f32[128,512]{1,0:T(8,128)} copy(f32[128,512]{1,0:T(8,128)S(1)} %get-tuple-element.5) | data formatting | bytes 524288
Async XLA Ops:
  0.6 0.7 %copy-start.4 = (s32[128]{0:T(128)S(1)}, s32[128]{0:T(128)}, u32[]{:S(2)}) copy-start(s32[128]{0:T(128)} %param.9) | copy-start | bytes 1540
  1.3 0.9 %copy-start = (bf16[128,512]{1,0:T(8,128)(2,1)S(1)}, bf16[128,512]{1,0:T(8,128)(2,1)}, u32[]{:S(2)}) copy-start(bf16[128,512]{1,0:T(8,128)(2,1)} %qt_ref.1) | copy-start | bytes 393220
  2.2 0.9 %copy-start.1 = (bf16[128,512]{1,0:T(8,128)(2,1)S(1)}, bf16[128,512]{1,0:T(8,128)(2,1)}, u32[]{:S(2)}) copy-start(bf16[128,512]{1,0:T(8,128)(2,1)} %kt_ref.1) | copy-start | bytes 393220
  3.1 0.9 %copy-start.2 = (bf16[128,512]{1,0:T(8,128)(2,1)S(1)}, bf16[128,512]{1,0:T(8,128)(2,1)}, u32[]{:S(2)}) copy-start(bf16[128,512]{1,0:T(8,128)(2,1)} %qs_ref.1) | copy-start | bytes 393220
  4.0 0.9 %copy-start.3 = (bf16[128,512]{1,0:T(8,128)(2,1)S(1)}, bf16[128,512]{1,0:T(8,128)(2,1)}, u32[]{:S(2)}) copy-start(bf16[128,512]{1,0:T(8,128)(2,1)} %ks_ref.1) | copy-start | bytes 393220

commit v2 on v1

--- a/solution.py
+++ b/solution.py
@@ -14,6 +14,7 @@
 LOWEST = -1e30
 INV_ROOT = HEAD_DIM ** (-0.5)
 MESH = pl.DeviceIdType.MESH
+ORDER = (3, 2, 1)
 
 
 def kernel(
@@ -21,7 +22,7 @@
     qt_ref, kt_ref, qs_ref, ks_ref, pos_ref,
     dq_ref, dk_ref,
     ktb, ksb, qtb, qsb, posb,
-    acc, dq_out, dq_in, dk_out, dk_in, part_out, part_in,
+    teacher, acc, dq_out, dk_out, part_out, part_in,
     local_sem, send_sem, recv_sem, fsend, frecv, psend, precv,
     dqs, dqr, dks, dkr,
 ):
@@ -41,10 +42,18 @@
     def mate(place):
         return {"outer": o, "blk": z0 + place}
 
+    def partner(k):
+        place = r
+        if k % 2:
+            place = place + 1 - 2 * lax.rem(place, 2)
+        if k // 2:
+            place = place + 2 - 4 * (place // 2)
+        return place
+
     barrier = pltpu.get_barrier_semaphore()
     for k in range(1, HEADS):
         pl.semaphore_signal(
-            barrier, inc=1, device_id=mate(lax.rem(r + k, HEADS)), device_id_type=MESH
+            barrier, inc=1, device_id=mate(partner(k)), device_id_type=MESH
         )
     for p in range(1, prior + 1):
         @pl.when(line >= HEADS * p)
@@ -96,7 +105,7 @@
     pl.semaphore_wait(barrier, HEADS - 1 + before + after)
 
     def outgoing(k, a):
-        place = lax.rem(r + k, HEADS)
+        place = partner(k)
         src, dst = routes(place, r)[a]
         return pltpu.make_async_remote_copy(
             src_ref=src, dst_ref=dst, send_sem=send_sem.at[k - 1, a], recv_sem=recv_sem.at[r, a],
@@ -104,7 +113,7 @@
         )
 
     def incoming(k, a):
-        place = lax.rem(r + k, HEADS)
+        place = partner(k)
         src, dst = routes(r, place)[a]
         return pltpu.make_async_remote_copy(
             src_ref=src, dst_ref=dst, send_sem=send_sem.at[k - 1, a],
@@ -112,13 +121,13 @@
             device_id=mate(place), device_id_type=MESH,
         )
 
-    for group in ((0, 1), (2, 3, 4)):
-        for k in range(1, HEADS):
-            for a in group:
+    for group in ((0, 4, 2), (1,), (3,)):
+        for a in group:
+            for k in ORDER:
                 outgoing(k, a).start()
 
     def forward(p, k, a, target):
-        place = lax.rem(r + k, HEADS)
+        place = partner(k)
         buf = (ktb, ksb)[a]
         there = pl.ds(
             pl.multiple_of((prior - p) * team_rows + place * rows, rows), rows
@@ -129,32 +138,34 @@
             device_id=at(target), device_id_type=MESH,
         )
 
-    def forward_all(k):
+    def forward_all(k, a):
         for p in range(1, prior + 1):
             @pl.when(line + HEADS * p < total)
             def _():
-                for a in range(2):
-                    forward(p, k, a, line + HEADS * p).start()
-
-    locals_[0].wait()
-    locals_[1].wait()
-    forward_all(0)
-    acc[...] = jnp.zeros_like(acc)
-    for copy in locals_[2:]:
-        copy.wait()
-    for k in range(1, HEADS):
-        incoming(k, 0).wait_recv()
-        incoming(k, 1).wait_recv()
-        forward_all(k)
-    for k in range(1, HEADS):
-        for a in (2, 3, 4):
+                forward(p, k, a, line + HEADS * p).start()
+
+    def forwarded(a):
+        for p in range(1, prior + 1):
+            @pl.when(line >= HEADS * p)
+            def _():
+                for k in range(HEADS):
+                    forward(p, k, a, line - HEADS * p).wait_recv()
+
+    def arrive(a):
+        for k in ORDER:
             incoming(k, a).wait_recv()
-    for p in range(1, prior + 1):
-        @pl.when(line >= HEADS * p)
-        def _():
-            for k in range(HEADS):
-                for a in range(2):
-                    forward(p, k, a, line - HEADS * p).wait_recv()
+            if a < 2:
+                forward_all(k, a)
+
+    for a in (0, 1):
+        locals_[a].wait()
+        forward_all(0, a)
+    for a in (2, 3, 4):
+        locals_[a].wait()
+    arrive(0)
+    arrive(4)
+    arrive(2)
+    forwarded(0)
 
     def send_part(block, target):
         p = prior - block // HEADS
@@ -173,22 +184,22 @@
             part_out[block] = acc[block * rows : (block + 1) * rows, :].astype(jnp.bfloat16)
             send_part(block, line - HEADS * p).start()
 
-    def result(out, into, send, recv, place, head):
-        return pltpu.make_async_remote_copy(
-            src_ref=out.at[place], dst_ref=into.at[head],
+    def result(out, ref, send, recv, place, head):
+        return pltpu.make_async_remote_copy(
+            src_ref=out.at[place], dst_ref=ref.at[:, cols(head)],
             send_sem=send.at[place], recv_sem=recv.at[head],
             device_id=mate(place), device_id_type=MESH,
         )
 
-    def give(i, value, ref, out, into, send, recv):
+    def give(i, value, ref, out, send, recv):
         @pl.when(r == i)
         def _():
-            ref[:, cols(r)] = value
+            ref[:, cols(r)] = value.astype(jnp.bfloat16)
 
         @pl.when(r != i)
         def _():
             out[i] = value.astype(jnp.bfloat16)
-            result(out, into, send, recv, i, r).start()
+            result(out, ref, send, recv, i, r).start()
 
     ahead = lax.broadcasted_iota(jnp.int32, (window, rows), 0) - lax.broadcasted_iota(
         jnp.int32, (window, rows), 1
@@ -204,22 +215,34 @@
         raised = jnp.exp2((masked - top) * power)
         return raised, LOSS_SCALE / jnp.sum(raised, axis=0, keepdims=True)
 
+    def seen(i):
+        return (ahead <= 0) & (ahead >= -posb[i])
+
     for i in range(HEADS):
         lo = i * rows
-        seen = (ahead <= 0) & (ahead >= -posb[i])
+        raised, scale = weights(ktb[lo : lo + window, :], qtb[lo : lo + rows, :], seen(i))
+        teacher[i] = raised * scale
+    arrive(1)
+    forwarded(1)
+    arrive(3)
+
+    for i in range(HEADS):
+        lo = i * rows
         queries = qsb[lo : lo + rows, :]
         keys = ksb[lo : lo + window, :]
-        t_raised, t_scale = weights(ktb[lo : lo + window, :], qtb[lo : lo + rows, :], seen)
-        s_raised, s_scale = weights(keys, queries, seen)
-        grad = (s_raised * s_scale - t_raised * t_scale).astype(jnp.bfloat16)
-        acc[lo : lo + window, :] += jnp.dot(
-            grad, queries, preferred_element_type=jnp.float32
-        ) * INV_ROOT
-        return_part(i)
+        raised, scale = weights(keys, queries, seen(i))
+        grad = (raised * scale - teacher[i]).astype(jnp.bfloat16)
         dq = lax.dot_general(
             grad, keys, (((0,), (0,)), ((), ())), preferred_element_type=jnp.float32
         ) * INV_ROOT
-        give(i, dq, dq_ref, dq_out, dq_in, dqs, dqr)
+        give(i, dq, dq_ref, dq_out, dqs, dqr)
+        dk = jnp.dot(grad, queries, preferred_element_type=jnp.float32) * INV_ROOT
+        if i == 0:
+            acc[0:window, :] = dk
+        else:
+            acc[lo : lo + window - rows, :] += dk[: window - rows]
+            acc[lo + window - rows : lo + window, :] = dk[window - rows :]
+        return_part(i)
     for block in range(HEADS, blk):
         return_part(block)
 
@@ -231,24 +254,20 @@
                 lo = own + j * rows
                 acc[lo : lo + rows, :] += part_in[p - 1, j].astype(jnp.float32)
         give(
-            j, acc[own + j * rows : own + (j + 1) * rows, :], dk_ref, dk_out, dk_in, dks, dkr
-        )
-
-    for ref, out, into, send, recv in (
-        (dq_ref, dq_out, dq_in, dqs, dqr),
-        (dk_ref, dk_out, dk_in, dks, dkr),
-    ):
-        for k in range(1, HEADS):
-            place = lax.rem(r + k, HEADS)
-            result(out, into, send, recv, place, place).wait_recv()
-            ref[:, cols(place)] = into[place].astype(jnp.float32)
+            j, acc[own + j * rows : own + (j + 1) * rows, :], dk_ref, dk_out, dks, dkr
+        )
+
+    for k in ORDER:
+        place = partner(k)
+        result(dq_out, dq_ref, dqs, dqr, place, place).wait_recv()
+        result(dk_out, dk_ref, dks, dkr, place, place).wait_recv()
 
     for k in range(1, HEADS):
         for a in range(5):
             outgoing(k, a).wait_send()
-        place = lax.rem(r + k, HEADS)
-        result(dq_out, dq_in, dqs, dqr, place, r).wait_send()
-        result(dk_out, dk_in, dks, dkr, place, r).wait_send()
+        place = partner(k)
+        result(dq_out, dq_ref, dqs, dqr, place, r).wait_send()
+        result(dk_out, dk_ref, dks, dkr, place, r).wait_send()
     for p in range(1, prior + 1):
         @pl.when(line + HEADS * p < total)
         def _():
@@ -272,10 +291,10 @@
     tile = (rows, HEAD_DIM)
     dma = pltpu.SemaphoreType.DMA
     pairs = HEADS * (span * rows) * HEAD_DIM
-    return pl.pallas_call(
+    grads = pl.pallas_call(
         functools.partial(kernel, blk, total, rows),
-        out_shape=[jax.ShapeDtypeStruct((rows, width), f32)] * 2,
-        in_specs=[pl.BlockSpec(memory_space=pl.ANY)] * 5,
+        out_shape=[jax.ShapeDtypeStruct((rows, width), bf16)] * 2,
+        in_specs=[pl.BlockSpec(memory_space=pltpu.HBM)] * 5,
         out_specs=[pl.BlockSpec(memory_space=pltpu.VMEM)] * 2,
         scratch_shapes=[
             pltpu.VMEM((span, HEAD_DIM), bf16),
@@ -283,9 +302,8 @@
             pltpu.VMEM((HEADS * rows, HEAD_DIM), bf16),
             pltpu.VMEM((HEADS * rows, HEAD_DIM), bf16),
             pltpu.VMEM((HEADS, 1, rows), jnp.int32),
+            pltpu.VMEM((HEADS, (blk + 1) * rows, rows), f32),
             pltpu.VMEM((span, HEAD_DIM), f32),
-            pltpu.VMEM((HEADS,) + tile, bf16),
-            pltpu.VMEM((HEADS,) + tile, bf16),
             pltpu.VMEM((HEADS,) + tile, bf16),
             pltpu.VMEM((HEADS,) + tile, bf16),
             pltpu.VMEM((blk,) + tile, bf16),
@@ -303,12 +321,13 @@
             dma((HEADS,)),
         ],
         compiler_params=pltpu.CompilerParams(
-            collective_id=0, has_side_effects=True, vmem_limit_bytes=32 * 1024 * 1024
+            collective_id=0, has_side_effects=True, vmem_limit_bytes=60 * 1024 * 1024
         ),
         cost_estimate=pl.CostEstimate(
             flops=8 * pairs, bytes_accessed=10 * rows * width * 2, transcendentals=2 * pairs // HEAD_DIM
         ),
     )(q_teacher, k_teacher, q_student, k_student, positions.reshape(1, rows))
+    return tuple(grad.astype(f32) for grad in grads)
 
 
 def solution(mesh):

time: 32.6 us -> 30.1 us (0.923)
  local copies, waits for them, and re-layouts: 5.67 us -> 0.01 us
  other arithmetic: 0 us -> 2.4 us
  Pallas kernels: 26.1 us -> 26.9 us
    unnamed x12 -> x2, local copies, waits for them, and re-layouts: 5.67 us -> 0.01 us
    convert_element_type x0 -> x2, other arithmetic: none -> 2.4 us  [body(): return tuple((grad.astype(f32) for grad in grads))]
    pallas_call x1, Pallas kernels: 26.1 us -> 26.9 us  [body(): pl.pallas_call(functools.partial(kernel, blk, total, rows), out_shape=[ja...]
where the time goes in v2:
time: 30.1 us; the launch traced here: 29.9 us
  Pallas kernels  26.9 us (89%)
  other arithmetic  2.4 us (8%)
  between operations  0.65 us (2%)
    pallas_call x1, Pallas kernels, body(): pl.pallas_call(functools.partial(kernel, blk, total, rows), out_shape=[ja...  26.9 us
    convert_element_type x2, other arithmetic, body(): return tuple((grad.astype(f32) for grad in grads))  2.4 us

profile of v2, /device:TPU:0, one launch (start us, length us, event | category | flops | bytes accessed | tf_op | source)
XLA Modules:
  0.0 29.9 jit_solution(11677458041256840116)
XLA Ops:
  0.6 26.9 %shard_map.68 = (bf16[128,512]{1,0:T(8,128)(2,1)}, bf16[128,512]{1,0:T(8,128)(2,1)}) custom-call(bf16[128,512]{1,0:T(8,128)(2,1)} %qt_ref.1, bf16[128,512]{1,0:T(8,128)(2,1)} %kt_ref.1, bf16[128,512]{1,0:T(8,128)(2,1)} %qs_ref.1, bf16[128,512]{1,0:T(8,128)(2,1)} %ks_ref.1, s32[1,128]{1,0:T(1,128)} %bitcast.1), custom_call_target="tpu_custom_call" | custom-call | flops 536870912 | bytes 1310720 | tf_op jit(solution)/shard_map/pallas_call | solution.py:294
  27.5 0.0 copy-start
  27.5 1.7 %convert_element_type.6 = f32[128,512]{1,0:T(8,128)} convert(bf16[128,512]{1,0:T(8,128)(2,1)} %get-tuple-element.4) | non-fusion elementwise | flops 65536 | bytes 393216 | tf_op jit(solution)/shard_map/convert_element_type | solution.py:330
  29.2 0.0 copy-done
  29.2 0.7 %convert_element_type.7 = f32[128,512]{1,0:T(8,128)} convert(bf16[128,512]{1,0:T(8,128)(2,1)S(1)} %copy-done) | non-fusion elementwise | flops 65536 | bytes 393216 | tf_op jit(solution)/shard_map/convert_element_type | solution.py:330
Async XLA Ops:
  27.5 1.7 %copy-start = (bf16[128,512]{1,0:T(8,128)(2,1)S(1)}, bf16[128,512]{1,0:T(8,128)(2,1)}, u32[]{:S(2)}) copy-start(bf16[128,512]{1,0:T(8,128)(2,1)} %get-tuple-element.5) | copy-start | bytes 393220

commit v3 on v2

--- a/solution.py
+++ b/solution.py
@@ -279,6 +279,11 @@
         def _():
             for j in range(HEADS):
                 send_part((prior - p) * HEADS + j, line - HEADS * p).wait_send()
+
+
+def widen(dq_ref, dk_ref, dq_wide, dk_wide):
+    dq_wide[...] = dq_ref[...].astype(jnp.float32)
+    dk_wide[...] = dk_ref[...].astype(jnp.float32)
 
 
 def body(q_teacher, k_teacher, q_student, k_student, positions):
@@ -327,7 +332,12 @@
             flops=8 * pairs, bytes_accessed=10 * rows * width * 2, transcendentals=2 * pairs // HEAD_DIM
         ),
     )(q_teacher, k_teacher, q_student, k_student, positions.reshape(1, rows))
-    return tuple(grad.astype(f32) for grad in grads)
+    return pl.pallas_call(
+        widen,
+        out_shape=[jax.ShapeDtypeStruct((rows, width), f32)] * 2,
+        in_specs=[pl.BlockSpec(memory_space=pltpu.VMEM)] * 2,
+        out_specs=[pl.BlockSpec(memory_space=pltpu.VMEM)] * 2,
+    )(*grads)
 
 
 def solution(mesh):

time: 30.1 us -> 29.5 us (0.980)
  other arithmetic: 2.4 us -> 0 us
  Pallas kernels: 26.9 us -> 28.7 us
    convert_element_type x2 -> x0, other arithmetic: 2.4 us -> none  [body(): return tuple((grad.astype(f32) for grad in grads))]
    pallas_call x0 -> x1, Pallas kernels: none -> 1.78 us  [body(): pl.pallas_call(widen, out_shape=[jax.ShapeDtypeStruct((rows, width), f32)...]
where the time goes in v3:
time: 29.5 us; the launch traced here: 29.3 us
  Pallas kernels  28.7 us (97%)
  between operations  0.64 us (2%)
    pallas_call x1, Pallas kernels, body(): pl.pallas_call(functools.partial(kernel, blk, total, rows), out_shape=[ja...  26.9 us
    pallas_call x1, Pallas kernels, body(): pl.pallas_call(widen, out_shape=[jax.ShapeDtypeStruct((rows, width), f32)...  1.78 us

profile of v3, /device:TPU:0, one launch (start us, length us, event | category | flops | bytes accessed | tf_op | source)
XLA Modules:
  0.0 29.3 jit_solution(17805911267142764119)
XLA Ops:
  0.6 26.9 %shard_map.68 = (bf16[128,512]{1,0:T(8,128)(2,1)}, bf16[128,512]{1,0:T(8,128)(2,1)}) custom-call(bf16[128,512]{1,0:T(8,128)(2,1)} %qt_ref.1, bf16[128,512]{1,0:T(8,128)(2,1)} %kt_ref.1, bf16[128,512]{1,0:T(8,128)(2,1)} %qs_ref.1, bf16[128,512]{1,0:T(8,128)(2,1)} %ks_ref.1, s32[1,128]{1,0:T(1,128)} %bitcast.1), custom_call_target="tpu_custom_call" | custom-call | flops 536870912 | bytes 1310720 | tf_op jit(solution)/shard_map/pallas_call | solution.py:299
  27.5 1.8 %shard_map.69 = (f32[128,512]{1,0:T(8,128)}, f32[128,512]{1,0:T(8,128)}) custom-call(bf16[128,512]{1,0:T(8,128)(2,1)} %get-tuple-element.4.dq_ref, bf16[128,512]{1,0:T(8,128)(2,1)} %get-tuple-element.5.dk_ref), custom_call_target="tpu_custom_call" | custom-call | tf_op jit(solution)/shard_map/pallas_call | solution.py:335

commit v4 on v3

--- a/solution.py
+++ b/solution.py
@@ -224,10 +224,18 @@
         teacher[i] = raised * scale
     arrive(1)
     forwarded(1)
-    arrive(3)
 
     for i in range(HEADS):
         lo = i * rows
+
+        @pl.when(r != i)
+        def _():
+            src, dst = routes(r, i)[3]
+            pltpu.make_async_remote_copy(
+                src_ref=src, dst_ref=dst, send_sem=send_sem.at[0, 3], recv_sem=recv_sem.at[i, 3],
+                device_id=mate(i), device_id_type=MESH,
+            ).wait_recv()
+
         queries = qsb[lo : lo + rows, :]
         keys = ksb[lo : lo + window, :]
         raised, scale = weights(keys, queries, seen(i))

time: 29.5 us -> 29.1 us (0.986)
  the two profiles are of different devices: /device:TPU:0 before, /device:TPU:1 now
where the time goes in v4:
time: 29.1 us; the launch traced here: 28.9 us
  Pallas kernels  28.3 us (97%)
  between operations  0.64 us (2%)
    pallas_call x1, Pallas kernels, body(): pl.pallas_call(functools.partial(kernel, blk, total, rows), out_shape=[ja...  26.5 us
    pallas_call x1, Pallas kernels, body(): pl.pallas_call(widen, out_shape=[jax.ShapeDtypeStruct((rows, width), f32)...  1.78 us

profile of v4, /device:TPU:1, one launch (start us, length us, event | category | flops | bytes accessed | tf_op | source)
XLA Modules:
  0.0 28.9 jit_solution(13377477600454945603)
XLA Ops:
  0.6 26.5 %shard_map.68 = (bf16[128,512]{1,0:T(8,128)(2,1)}, bf16[128,512]{1,0:T(8,128)(2,1)}) custom-call(bf16[128,512]{1,0:T(8,128)(2,1)} %qt_ref.1, bf16[128,512]{1,0:T(8,128)(2,1)} %kt_ref.1, bf16[128,512]{1,0:T(8,128)(2,1)} %qs_ref.1, bf16[128,512]{1,0:T(8,128)(2,1)} %ks_ref.1, s32[1,128]{1,0:T(1,128)} %bitcast.1), custom_call_target="tpu_custom_call" | custom-call | flops 536870912 | bytes 1310720 | tf_op jit(solution)/shard_map/pallas_call | solution.py:307
  27.2 1.8 %shard_map.69 = (f32[128,512]{1,0:T(8,128)}, f32[128,512]{1,0:T(8,128)}) custom-call(bf16[128,512]{1,0:T(8,128)(2,1)} %get-tuple-element.4.dq_ref, bf16[128,512]{1,0:T(8,128)(2,1)} %get-tuple-element.5.dk_ref), custom_call_target="tpu_custom_call" | custom-call | tf_op jit(solution)/shard_map/pallas_call | solution.py:343
